TPU v7x, 128 devices: a whole 4x4x4 slice. The times are simulated.
128 devices in a mesh: seq: 16 (over z, y_lo, core), chan: 8 (over y_hi, x).
Axes of the slice: x: 4, y: 4 (y_hi: 2, y_lo: 2; y = y_hi * 2 + y_lo), z: 4, core: 2. Of those that a mesh axis runs over, the one named last changes fastest.
Arguments:
- inputs: bfloat16 [16384, 4096], P('seq', 'chan'), may hold values from -6 to 6
- out_grad: bfloat16 [16384, 4096], P('seq', 'chan'), may hold values from -6 to 6
- out_weight: bfloat16 [4096, 4096], P('chan'), may hold values from -0.09375 to 0.09375
- filt: float32 [2048, 4096], P('seq', 'chan'), may hold values from -1.2 to 1.2
Outputs:
- grad_in: bfloat16 [16384, 4096], P('seq', 'chan')
- filt_grad: float32 [2048, 4096], P('seq', 'chan')
All inputs are finite; a program needn't handle non-finite values.
Results may differ from a plain program's by a relative error of at most 0.0049.
Values may be sent and summed in bfloat16 or wider, within the bound.
A program may use at most 256 MiB of HBM per device.

v0:
```python
import math
import jax
import jax.numpy as jnp
from jax import lax
from jax.sharding import PartitionSpec as P

LAG_STEPS = 2
BLOCK = 256
highest = lax.Precision.HIGHEST
higher = lax.Precision.HIGH


def from_behind(block, axis, distance):
    devices = range(lax.axis_size(axis))
    route = [(i - distance, i) for i in devices if i - distance in devices]
    return lax.ppermute(block, axis, route)


def per_device(inputs, out_grad, out_weight, filt):
    span_len, chan_width = inputs.shape
    block_len = BLOCK
    frame_len = 2 * BLOCK
    mixed_sum = lax.dot_general(
        lax.all_gather(out_grad, "chan", axis=1, tiled=True),
        out_weight,
        (((1,), (1,)), ((), ())),
        preferred_element_type=jnp.float32,
    )
    grad_mix = mixed_sum.astype(jnp.bfloat16)
    whole_filter = lax.all_gather(filt, "seq", axis=0, tiled=True)
    later_list = [from_behind(grad_mix, "seq", -offset) for offset in range(1, LAG_STEPS + 1)]
    extended = jnp.concatenate([grad_mix] + later_list, axis=0)
    freq_index = lax.iota(jnp.int32, frame_len)[:, None]
    time_index = lax.iota(jnp.int32, block_len)[None, :]
    angles = (freq_index * time_index % frame_len).astype(jnp.float32) * (2.0 * math.pi / frame_len)
    cos_table = jnp.cos(angles)
    sin_table = jnp.sin(angles)
    parity = jnp.where(lax.iota(jnp.int32, frame_len) % 2 == 0, 1.0, -1.0).astype(jnp.float32)[
        None, :, None
    ]

    def spectrum(blocks, level):
        real_part = jnp.einsum("fb,nbc->nfc", cos_table, blocks, precision=level)
        imag_part = -jnp.einsum("fb,nbc->nfc", sin_table, blocks, precision=level)
        return (real_part, imag_part)

    def inverse(real_part, imag_part):
        front = jnp.einsum("fa,nfc->nac", cos_table, real_part, precision=highest)
        back = jnp.einsum("fa,nfc->nac", sin_table, imag_part, precision=highest)
        return (front - back) / frame_len

    base_real, base_imag = spectrum(
        extended.astype(jnp.float32).reshape(-1, block_len, chan_width), higher
    )
    win_real = base_real[:-1] + parity * base_real[1:]
    win_imag = base_imag[:-1] + parity * base_imag[1:]
    lag_real, lag_imag = spectrum(whole_filter.reshape(-1, block_len, chan_width), highest)
    val_real, val_imag = spectrum(
        inputs.astype(jnp.float32).reshape(-1, block_len, chan_width), higher
    )
    lag_count = lag_real.shape[0]
    block_count = val_real.shape[0]

    def add_lag(lag_index, totals):
        slice_real = lax.dynamic_slice_in_dim(win_real, lag_index, block_count, 0)
        slice_imag = lax.dynamic_slice_in_dim(win_imag, lag_index, block_count, 0)
        coef_real = lax.dynamic_index_in_dim(lag_real, lag_index, 0, keepdims=False)
        coef_imag = lax.dynamic_index_in_dim(lag_imag, lag_index, 0, keepdims=False)
        return (
            totals[0] + coef_real * slice_real + coef_imag * slice_imag,
            totals[1] + coef_real * slice_imag - coef_imag * slice_real,
        )

    empty_in = jnp.zeros((block_count, frame_len, chan_width), jnp.float32)
    sum_real, sum_imag = lax.fori_loop(0, lag_count, add_lag, (empty_in, empty_in))

    def add_block(block_index, totals):
        slice_real = lax.dynamic_slice_in_dim(win_real, block_index, lag_count, 0)
        slice_imag = lax.dynamic_slice_in_dim(win_imag, block_index, lag_count, 0)
        coef_real = lax.dynamic_index_in_dim(val_real, block_index, 0, keepdims=False)
        coef_imag = lax.dynamic_index_in_dim(val_imag, block_index, 0, keepdims=False)
        return (
            totals[0] + coef_real * slice_real + coef_imag * slice_imag,
            totals[1] + coef_real * slice_imag - coef_imag * slice_real,
        )

    empty_lag = jnp.zeros((lag_count, frame_len, chan_width), jnp.float32)
    grad_real, grad_imag = lax.fori_loop(0, block_count, add_block, (empty_lag, empty_lag))
    grad_in = inverse(sum_real, sum_imag).reshape(span_len, chan_width).astype(jnp.bfloat16)
    local_grad = inverse(grad_real, grad_imag).reshape(-1, chan_width)
    seq_count = lax.axis_size("seq")
    grad_scale = 1.0 / math.sqrt(span_len * seq_count)
    owned = lax.psum_scatter(local_grad, "seq", scatter_dimension=0, tiled=True)
    filt_grad = owned * grad_scale
    return (grad_in, filt_grad)


def solution(mesh):
    in_specs = (P("seq", "chan"), P("seq", "chan"), P("chan", None), P("seq", "chan"))
    out_specs = (P("seq", "chan"), P("seq", "chan"))
    return jax.shard_map(
        per_device, mesh=mesh, in_specs=in_specs, out_specs=out_specs, check_vma=False
    )
```

profile of v0, /device:TPU:3, one launch (start us, length us, event | category | flops | bytes accessed | tf_op | source)
XLA Modules:
  0.0 510.7 jit_solution(2675074448289331453)
XLA Ops:
  7.2 0.7 all-gather.5.cloned.1.call-update
  8.0 0.7 all-gather.3.cloned.1.call-update
  8.7 123.2 %all-gather.5.cloned.1.call-done = bf16[1024,4096]{1,0:T(8,128)(2,1)} async-done(((bf16[1024,512]{1,0:T(8,128)(2,1)}), bf16[1024,4096]{1,0:T(8,128)(2,1)}) %all-gather.5.cloned.1.call-update) | async-done | bytes 8388624 | tf_op jit(solution)/shard_map/all_gather | solution.py:24
  131.9 9.1 %convolution_convert_fusion = bf16[1024,512]{1,0:T(8,128)(2,1)S(1)} fusion(bf16[1024,4096]{1,0:T(8,128)(2,1)} %all-gather.5.cloned.1.call-done, bf16[512,4096]{1,0:T(8,128)(2,1)} %param.10), kind=kOutput, calls=%fused_computation.25 | convolution fusion | flops 4295491584 | bytes 13631488 | tf_op jit(solution)/shard_map/dot_general | solution.py:23
  141.0 3.4 collective-permute-start
  144.5 1.5 collective-permute-start.1
  146.0 4.7 convolution_bitcast_fusion.2
  150.7 4.7 negate_bitcast_fusion.2
  155.5 51.2 %all-gather.3.cloned.1.call-done = f32[2048,512]{1,0:T(8,128)} async-done(((f32[128,512]{1,0:T(8,128)}), f32[2048,512]{1,0:T(8,128)}) %all-gather.3.cloned.1.call-update) | async-done | bytes 4194320 | tf_op jit(solution)/shard_map/all_gather | solution.py:30
  206.6 14.5 %convolution_bitcast_fusion.1 = f32[8,512,512]{2,1,0:T(8,128)} fusion(f32[8,256,512]{2,1,0:T(8,128)} %bitcast.77), kind=kOutput, calls=%fused_computation.21 | convolution fusion | flops 6444285952 | bytes 12582912 | tf_op jit(solution)/shard_map/fb,nbc->nfc/dot_general | solution.py:43
  221.1 1.5 pad_maximum_fusion
  222.7 5.7 %convolution_bitcast_fusion = f32[12,512,512]{1,2,0:T(8,128)S(1)} fusion(bf16[12,256,512]{2,1,0:T(8,128)(2,1)S(1)} %bitcast.75), kind=kOutput, calls=%fused_computation.18 | convolution fusion | flops 4833673216 | bytes 15728640 | tf_op jit(solution)/shard_map/fb,nbc->nfc/dot_general | solution.py:43
  228.4 9.9 %negate_bitcast_fusion = f32[12,512,512]{1,2,0:T(8,128)} fusion(bf16[12,256,512]{2,1,0:T(8,128)(2,1)S(1)} %bitcast.76), kind=kOutput, calls=%fused_computation.12 | convolution fusion | flops 4836818944 | bytes 15728640 | tf_op jit(solution)/shard_map/fb,nbc->nfc/dot_general | solution.py:44
  238.3 16.4 %fusion.4 = (f32[11,512,512]{1,2,0:T(8,128)}, f32[11,512,512]{1,2,0:T(8,128)}) fusion(f32[12,512,512]{1,2,0:T(8,128)} %negate_bitcast_fusion, f32[512]{0:T(512)S(1)} %fusion.39, f32[12,512,512]{1,2,0:T(8,128)S(1)} %convolution_bitcast_fusion), kind=kLoop, calls=%fused_computation.14 | loop fusion | flops 11534336 | bytes 69208064 | tf_op jit(solution)/shard_map/add | solution.py:56
  254.7 12.1 %copy.12 = f32[11,512,512]{2,1,0:T(8,128)} copy(f32[11,512,512]{1,2,0:T(8,128)} %get-tuple-element.355) | data formatting | bytes 23068672
  266.8 12.1 %copy.13 = f32[11,512,512]{2,1,0:T(8,128)} copy(f32[11,512,512]{1,2,0:T(8,128)} %get-tuple-element.354) | data formatting | bytes 23068672
  279.0 77.0 %while.33 = (s32[]{:T(128)}, f32[8,512,512]{2,1,0:T(8,128)}, f32[8,512,512]{2,1,0:T(8,128)}, f32[4,512,512]{2,1,0:T(8,128)}, f32[11,512,512]{2,1,0:T(8,128)}, /*...) while((s32[]{:T(128)}, f32[8,512,512]{2,1,0:T(8,128)}, ...), condition=%wide.region_3.4_spmd.clone, body=%wide.region_2.3_spmd.clone.sunk | while | flops 20971524 | bytes 56623212 | solution.py:88
  279.3 1.7 dynamic-slice_bitcast_fusion.7
  281.1 11.9 %fusion.96 = (f32[8,512,512]{2,1,0:T(8,128)}, f32[8,512,512]{2,1,0:T(8,128)}) fusion(f32[8,512,512]{2,1,0:T(8,128)} %get-tuple-element.496, f32[11,512,512]{2,1,0:T(8,128)} %get-tuple-element.509, s32[]{:T(128)} %get-tuple-element.494, f32[11,512,512]{2,1,0:T(8,128)} %get-tuple-element.507, f32[512,512]{1,0:T(8,128)S(1)} %get-tuple-element.454, ...), kind=kLoop, calls=%fused_computation.7.clone.1 | loop fusion | flops 20971520 | bytes 52428804 | tf_op jit(solution)/shard_map/while/body/eval_jaxpr/sub | solution.py:84
  293.0 1.7 dynamic-slice_bitcast_fusion.7
  294.7 19.3 %fusion.96 = (f32[8,512,512]{2,1,0:T(8,128)}, f32[8,512,512]{2,1,0:T(8,128)}) fusion(f32[8,512,512]{2,1,0:T(8,128)} %get-tuple-element.496, f32[11,512,512]{2,1,0:T(8,128)} %get-tuple-element.509, s32[]{:T(128)} %get-tuple-element.494, f32[11,512,512]{2,1,0:T(8,128)} %get-tuple-element.507, f32[512,512]{1,0:T(8,128)S(1)} %get-tuple-element.454, ...), kind=kLoop, calls=%fused_computation.7.clone.1 | loop fusion | flops 20971520 | bytes 52428804 | tf_op jit(solution)/shard_map/while/body/eval_jaxpr/sub | solution.py:84
  314.0 1.7 dynamic-slice_bitcast_fusion.7
  315.7 19.3 %fusion.96 = (f32[8,512,512]{2,1,0:T(8,128)}, f32[8,512,512]{2,1,0:T(8,128)}) fusion(f32[8,512,512]{2,1,0:T(8,128)} %get-tuple-element.496, f32[11,512,512]{2,1,0:T(8,128)} %get-tuple-element.509, s32[]{:T(128)} %get-tuple-element.494, f32[11,512,512]{2,1,0:T(8,128)} %get-tuple-element.507, f32[512,512]{1,0:T(8,128)S(1)} %get-tuple-element.454, ...), kind=kLoop, calls=%fused_computation.7.clone.1 | loop fusion | flops 20971520 | bytes 52428804 | tf_op jit(solution)/shard_map/while/body/eval_jaxpr/sub | solution.py:84
  335.0 1.7 dynamic-slice_bitcast_fusion.7
  336.7 19.3 %fusion.96 = (f32[8,512,512]{2,1,0:T(8,128)}, f32[8,512,512]{2,1,0:T(8,128)}) fusion(f32[8,512,512]{2,1,0:T(8,128)} %get-tuple-element.496, f32[11,512,512]{2,1,0:T(8,128)} %get-tuple-element.509, s32[]{:T(128)} %get-tuple-element.494, f32[11,512,512]{2,1,0:T(8,128)} %get-tuple-element.507, f32[512,512]{1,0:T(8,128)S(1)} %get-tuple-element.454, ...), kind=kLoop, calls=%fused_computation.7.clone.1 | loop fusion | flops 20971520 | bytes 52428804 | tf_op jit(solution)/shard_map/while/body/eval_jaxpr/sub | solution.py:84
  356.0 14.5 %fusion.15 = f32[8,512,256]{1,2,0:T(8,128)S(1)} fusion(f32[8,512,512]{2,1,0:T(8,128)} %get-tuple-element.254), kind=kOutput, calls=%fused_computation.38 | convolution fusion | flops 6444285952 | bytes 12582912 | tf_op jit(solution)/shard_map/fa,nfc->nac/dot_general | solution.py:48
  370.5 13.7 %subtract_multiply_fusion = f32[8,512,256]{1,2,0:T(8,128)} fusion(f32[8,512,256]{1,2,0:T(8,128)S(1)} %fusion.15, f32[8,512,512]{2,1,0:T(8,128)S(1)} %copy-done.2), kind=kOutput, calls=%fused_computation.19 | convolution fusion | flops 6446383104 | bytes 16777216 | tf_op jit(solution)/shard_map/fa,nfc->nac/dot_general | solution.py:49
  384.3 14.6 %negate_bitcast_fusion.1 = f32[8,512,512]{2,1,0:T(8,128)} fusion(f32[8,256,512]{2,1,0:T(8,128)} %bitcast.78), kind=kOutput, calls=%fused_computation.17 | convolution fusion | flops 6446383104 | bytes 12582912 | tf_op jit(solution)/shard_map/fb,nbc->nfc/dot_general | solution.py:44
  398.9 88.1 %while.32 = (s32[]{:T(128)}, f32[4,512,512]{2,1,0:T(8,128)}, f32[4,512,512]{2,1,0:T(8,128)}, f32[8,512,512]{2,1,0:T(8,128)}, f32[11,512,512]{2,1,0:T(8,128)}, /*...) while((s32[]{:T(128)}, f32[4,512,512]{2,1,0:T(8,128)}, ...), condition=%wide.region_1.2_spmd.clone, body=%wide.region_0.1_spmd.clone.sunk | while | flops 10485763 | bytes 31457388 | solution.py:75
  398.9 1.7 dynamic-slice_bitcast_fusion.6
  400.6 6.9 %fusion.95 = (f32[4,512,512]{2,1,0:T(8,128)}, f32[4,512,512]{2,1,0:T(8,128)}) fusion(f32[4,512,512]{2,1,0:T(8,128)} %get-tuple-element.469, f32[11,512,512]{2,1,0:T(8,128)} %get-tuple-element.482, s32[]{:T(128)} %get-tuple-element.467, f32[11,512,512]{2,1,0:T(8,128)} %get-tuple-element.480, f32[512,512]{1,0:T(8,128)S(1)} %get-tuple-element.443, ...), kind=kLoop, calls=%fused_computation.1.clone.1 | loop fusion | flops 10485760 | bytes 27262980 | tf_op jit(solution)/shard_map/while/body/eval_jaxpr/sub | solution.py:71
  407.5 1.7 dynamic-slice_bitcast_fusion.6
  409.3 9.6 %fusion.95 = (f32[4,512,512]{2,1,0:T(8,128)}, f32[4,512,512]{2,1,0:T(8,128)}) fusion(f32[4,512,512]{2,1,0:T(8,128)} %get-tuple-element.469, f32[11,512,512]{2,1,0:T(8,128)} %get-tuple-element.482, s32[]{:T(128)} %get-tuple-element.467, f32[11,512,512]{2,1,0:T(8,128)} %get-tuple-element.480, f32[512,512]{1,0:T(8,128)S(1)} %get-tuple-element.443, ...), kind=kLoop, calls=%fused_computation.1.clone.1 | loop fusion | flops 10485760 | bytes 27262980 | tf_op jit(solution)/shard_map/while/body/eval_jaxpr/sub | solution.py:71
  418.9 1.7 dynamic-slice_bitcast_fusion.6
  420.7 9.7 %fusion.95 = (f32[4,512,512]{2,1,0:T(8,128)}, f32[4,512,512]{2,1,0:T(8,128)}) fusion(f32[4,512,512]{2,1,0:T(8,128)} %get-tuple-element.469, f32[11,512,512]{2,1,0:T(8,128)} %get-tuple-element.482, s32[]{:T(128)} %get-tuple-element.467, f32[11,512,512]{2,1,0:T(8,128)} %get-tuple-element.480, f32[512,512]{1,0:T(8,128)S(1)} %get-tuple-element.443, ...), kind=kLoop, calls=%fused_computation.1.clone.1 | loop fusion | flops 10485760 | bytes 27262980 | tf_op jit(solution)/shard_map/while/body/eval_jaxpr/sub | solution.py:71
  430.4 1.7 dynamic-slice_bitcast_fusion.6
  432.2 9.7 %fusion.95 = (f32[4,512,512]{2,1,0:T(8,128)}, f32[4,512,512]{2,1,0:T(8,128)}) fusion(f32[4,512,512]{2,1,0:T(8,128)} %get-tuple-element.469, f32[11,512,512]{2,1,0:T(8,128)} %get-tuple-element.482, s32[]{:T(128)} %get-tuple-element.467, f32[11,512,512]{2,1,0:T(8,128)} %get-tuple-element.480, f32[512,512]{1,0:T(8,128)S(1)} %get-tuple-element.443, ...), kind=kLoop, calls=%fused_computation.1.clone.1 | loop fusion | flops 10485760 | bytes 27262980 | tf_op jit(solution)/shard_map/while/body/eval_jaxpr/sub | solution.py:71
  441.9 1.7 dynamic-slice_bitcast_fusion.6
  443.6 9.7 %fusion.95 = (f32[4,512,512]{2,1,0:T(8,128)}, f32[4,512,512]{2,1,0:T(8,128)}) fusion(f32[4,512,512]{2,1,0:T(8,128)} %get-tuple-element.469, f32[11,512,512]{2,1,0:T(8,128)} %get-tuple-element.482, s32[]{:T(128)} %get-tuple-element.467, f32[11,512,512]{2,1,0:T(8,128)} %get-tuple-element.480, f32[512,512]{1,0:T(8,128)S(1)} %get-tuple-element.443, ...), kind=kLoop, calls=%fused_computation.1.clone.1 | loop fusion | flops 10485760 | bytes 27262980 | tf_op jit(solution)/shard_map/while/body/eval_jaxpr/sub | solution.py:71
  453.3 1.7 dynamic-slice_bitcast_fusion.6
  455.0 9.4 %fusion.95 = (f32[4,512,512]{2,1,0:T(8,128)}, f32[4,512,512]{2,1,0:T(8,128)}) fusion(f32[4,512,512]{2,1,0:T(8,128)} %get-tuple-element.469, f32[11,512,512]{2,1,0:T(8,128)} %get-tuple-element.482, s32[]{:T(128)} %get-tuple-element.467, f32[11,512,512]{2,1,0:T(8,128)} %get-tuple-element.480, f32[512,512]{1,0:T(8,128)S(1)} %get-tuple-element.443, ...), kind=kLoop, calls=%fused_computation.1.clone.1 | loop fusion | flops 10485760 | bytes 27262980 | tf_op jit(solution)/shard_map/while/body/eval_jaxpr/sub | solution.py:71
  464.5 1.7 dynamic-slice_bitcast_fusion.6
  466.2 9.4 %fusion.95 = (f32[4,512,512]{2,1,0:T(8,128)}, f32[4,512,512]{2,1,0:T(8,128)}) fusion(f32[4,512,512]{2,1,0:T(8,128)} %get-tuple-element.469, f32[11,512,512]{2,1,0:T(8,128)} %get-tuple-element.482, s32[]{:T(128)} %get-tuple-element.467, f32[11,512,512]{2,1,0:T(8,128)} %get-tuple-element.480, f32[512,512]{1,0:T(8,128)S(1)} %get-tuple-element.443, ...), kind=kLoop, calls=%fused_computation.1.clone.1 | loop fusion | flops 10485760 | bytes 27262980 | tf_op jit(solution)/shard_map/while/body/eval_jaxpr/sub | solution.py:71
  475.6 1.7 dynamic-slice_bitcast_fusion.6
  477.4 9.4 %fusion.95 = (f32[4,512,512]{2,1,0:T(8,128)}, f32[4,512,512]{2,1,0:T(8,128)}) fusion(f32[4,512,512]{2,1,0:T(8,128)} %get-tuple-element.469, f32[11,512,512]{2,1,0:T(8,128)} %get-tuple-element.482, s32[]{:T(128)} %get-tuple-element.467, f32[11,512,512]{2,1,0:T(8,128)} %get-tuple-element.480, f32[512,512]{1,0:T(8,128)S(1)} %get-tuple-element.443, ...), kind=kLoop, calls=%fused_computation.1.clone.1 | loop fusion | flops 10485760 | bytes 27262980 | tf_op jit(solution)/shard_map/while/body/eval_jaxpr/sub | solution.py:71
  487.0 8.2 %fusion.17 = f32[4,512,256]{1,2,0:T(8,128)S(1)} fusion(f32[4,512,512]{2,1,0:T(8,128)} %get-tuple-element.252), kind=kOutput, calls=%fused_computation.40 | convolution fusion | flops 3223060480 | bytes 6291456 | tf_op jit(solution)/shard_map/fa,nfc->nac/dot_general | solution.py:48
  495.2 7.0 %multiply_convert_fusion = bf16[4,512,256]{1,2,0:T(8,128)(2,1)} fusion(f32[4,512,256]{1,2,0:T(8,128)S(1)} %fusion.17, f32[4,512,512]{2,1,0:T(8,128)S(1)} %copy-done.3), kind=kOutput, calls=%fused_computation.24 | convolution fusion | flops 3224633344 | bytes 7340032 | tf_op jit(solution)/shard_map/fa,nfc->nac/dot_general | solution.py:49
  502.2 1.7 broadcast_multiply_fusion
  (20 shorter events, 0.2 us)
Async XLA Ops:
  7.2 138.8 %copy-start = (bf16[1024,512]{1,0:T(8,128)(2,1)S(1)}, bf16[1024,512]{1,0:T(8,128)(2,1)}, u32[]{:S(2)}) copy-start(bf16[1024,512]{1,0:T(8,128)(2,1)} %param.8) | copy-start | bytes 3145732
  7.2 124.8 %all-gather.5.cloned.1.call-start = ((), (), s32[]{:S(2)}) async-start(), calls=%async_computation.2 | async-start | bytes 9437184 | tf_op jit(solution)/shard_map/all_gather | solution.py:24
  7.9 198.7 %all-gather.3.cloned.1.call-start = ((), (), s32[]{:S(2)}) async-start(), calls=%async_computation.1 | async-start | bytes 4456448 | tf_op jit(solution)/shard_map/all_gather | solution.py:30
  8.7 493.6 %reduce-scatter.2.cloned.1.call-start = ((), (), s32[]{:S(2)}) async-start(), calls=%async_computation.3 | async-start | bytes 4456448 | tf_op jit(solution)/shard_map/reduce_scatter | solution.py:93
  141.0 80.1 %collective-permute-start = (bf16[1024,512]{1,0:T(8,128)(2,1)S(1)}, bf16[1024,512]{1,0:T(8,128)(2,1)S(1)}, u32[]{:S(2)}, u32[]{:S(2)}) collective-permute-start(bf16[1024,512]{1,0:T(8,128)(2,1)S(1)} %convolution_convert_fusion), channel_id=1, source_target_pairs={{8,0},{16,8},{24,16},{32,24},{40,32},{48,40},{56,48},{64,56},{72,6... | collective-permute-start | bytes 3145736 | tf_op jit(solution)/shard_map/ppermute | solution.py:16
  144.5 76.6 %collective-permute-start.1 = (bf16[1024,512]{1,0:T(8,128)(2,1)S(1)}, bf16[1024,512]{1,0:T(8,128)(2,1)}, u32[]{:S(2)}, u32[]{:S(2)}) collective-permute-start(bf16[1024,512]{1,0:T(8,128)(2,1)S(1)} %convolution_convert_fusion), channel_id=1, source_target_pairs={{16,0},{24,8},{32,16},{40,24},{48,32},{56,40},{64,48},{72,56},{80,... | collective-permute-start | bytes 3145736 | tf_op jit(solution)/shard_map/ppermute | solution.py:16
  356.0 14.6 %copy-start.2 = (f32[8,512,512]{2,1,0:T(8,128)S(1)}, f32[8,512,512]{2,1,0:T(8,128)}, u32[]{:S(2)}) copy-start(f32[8,512,512]{2,1,0:T(8,128)} %get-tuple-element.255) | copy-start | bytes 25165828
  487.0 8.2 %copy-start.3 = (f32[4,512,512]{2,1,0:T(8,128)S(1)}, f32[4,512,512]{2,1,0:T(8,128)}, u32[]{:S(2)}) copy-start(f32[4,512,512]{2,1,0:T(8,128)} %get-tuple-element.253) | copy-start | bytes 12582916
  487.0 16.9 %copy-start.1 = (bf16[1024,512]{1,0:T(8,128)(2,1)S(1)}, bf16[1024,512]{1,0:T(8,128)(2,1)}, u32[]{:S(2)}) copy-start(bf16[1024,512]{1,0:T(8,128)(2,1)} %param.8) | copy-start | bytes 3145732
Sparse Core Ops, SparseCore 0:
  10.2 121.7 all-gather.4
  133.7 72.9 all-gather.2
  384.4 66.2 reduce-scatter.1
where the time goes:
time: 515 us; the launch traced here: 511 us
  waiting for transfers between devices  176 us (34%)
  other arithmetic  163 us (32%)
  matrix products  107 us (21%)
  local copies, waits for them, and re-layouts  45 us (9%)
  between operations  14.1 us (3%)
    all_gather x1, waiting for transfers between devices, per_device(): lax.all_gather(out_grad, 'chan', axis=1, tiled=True)  123 us
    sub x8, other arithmetic, add_lag(): totals[1] + coef_real * slice_imag - coef_imag * slice_real  74 us
    sub x4, other arithmetic, add_block(): totals[1] + coef_real * slice_imag - coef_imag * slice_real  69.7 us
    all_gather x1, waiting for transfers between devices, per_device(): whole_filter = lax.all_gather(filt, 'seq', axis=0, tiled=True)  51.2 us
    dot_general x3, matrix products, spectrum(): imag_part = -jnp.einsum('fb,nbc->nfc', sin_table, blocks, precision=level)  29.2 us
    dot_general x3, matrix products, spectrum(): real_part = jnp.einsum('fb,nbc->nfc', cos_table, blocks, precision=level)  24.9 us
    unnamed x10, local copies, waits for them, and re-layouts  24.3 us
    dot_general x2, matrix products, inverse(): front = jnp.einsum('fa,nfc->nac', cos_table, real_part, precision=highest)  22.7 us
  transfers between devices with their start and end apart: 5, of which 2 were waited for; matrix products, arithmetic and copies ran while one was open for 30% of the time, Pallas kernels for 0%

commit v1 on v0

--- a/solution.py
+++ b/solution.py
@@ -21,7 +21,9 @@
     block_len = BLOCK
     frame_len = 2 * BLOCK
     mixed_sum = lax.dot_general(
-        lax.all_gather(out_grad, "chan", axis=1, tiled=True),
+        jnp.concatenate(
+            lax.all_to_all(jnp.stack([out_grad] * lax.axis_size("chan")), "chan", 0, 0), axis=1
+        ),
         out_weight,
         (((1,), (1,)), ((), ())),
         preferred_element_type=jnp.float32,

time: 515 us -> 489 us (0.950)
  the two profiles are of different devices: /device:TPU:3 before, /device:TPU:30 now
where the time goes in v1:
time: 489 us; the launch traced here: 483 us
  other arithmetic  163 us (33%)
  waiting for transfers between devices  135 us (28%)
  matrix products  107 us (22%)
  local copies, waits for them, and re-layouts  50.9 us (10%)
  between operations  14.4 us (3%)
  starting transfers between devices  11.3 us (2%)
    all_to_all x1, waiting for transfers between devices, per_device(): lax.all_to_all(jnp.stack([out_grad] * lax.axis_size('chan')), 'chan', 0, 0)  123 us
    sub x8, other arithmetic, add_lag(): totals[1] + coef_real * slice_imag - coef_imag * slice_real  74 us
    sub x4, other arithmetic, add_block(): totals[1] + coef_real * slice_imag - coef_imag * slice_real  69.8 us
    dot_general x3, matrix products, spectrum(): imag_part = -jnp.einsum('fb,nbc->nfc', sin_table, blocks, precision=level)  29.3 us
    unnamed x11, local copies, waits for them, and re-layouts  25.9 us
    dot_general x3, matrix products, spectrum(): real_part = jnp.einsum('fb,nbc->nfc', cos_table, blocks, precision=level)  24.9 us
    dot_general x2, matrix products, inverse(): front = jnp.einsum('fa,nfc->nac', cos_table, real_part, precision=highest)  22.7 us
    dot_general x2, matrix products, inverse(): back = jnp.einsum('fa,nfc->nac', sin_table, imag_part, precision=highest)  20.8 us
  transfers between devices with their start and end apart: 5, of which 2 were waited for; matrix products, arithmetic and copies ran while one was open for 31% of the time, Pallas kernels for 0%

profile of v1, /device:TPU:30, one launch (start us, length us, event | category | flops | bytes accessed | tf_op | source)
XLA Modules:
  0.0 482.7 jit_solution(12264850332394792786)
XLA Ops:
  7.2 1.6 copy.19
  8.8 4.3 stack.2
  13.1 7.2 %all-to-all-start = ((bf16[8,1024,512]{1,2,0:T(8,128)(2,1)}), bf16[8,1024,512]{1,2,0:T(8,128)(2,1)}, u32[]{:S(2)}, u32[]{:S(2)}) async-start(bf16[8,1024,512]{1,2,0:T(8,128)(2,1)} %stack.2), calls=%async_computation | async-start | bytes 16777216 | tf_op jit(solution)/shard_map/all_to_all | solution.py:25
  21.0 123.4 %all-to-all-done = bf16[8,1024,512]{1,2,0:T(8,128)(2,1)} async-done(((bf16[8,1024,512]{1,2,0:T(8,128)(2,1)}), bf16[8,1024,512]{1,2,0:T(8,128)(2,1)}, u32[]{:S(2)}, u32[]{:S(2)}) %all-to-all-start) | async-done | bytes 8388640 | tf_op jit(solution)/shard_map/all_to_all | solution.py:25
  144.4 9.1 %convolution_convert_fusion = bf16[1024,512]{1,0:T(8,128)(2,1)S(1)} fusion(bf16[1024,4096]{0,1:T(8,128)(2,1)} %bitcast.4, bf16[512,4096]{1,0:T(8,128)(2,1)} %param.10), kind=kOutput, calls=%fused_computation.25 | convolution fusion | flops 4295491584 | bytes 13631488 | tf_op jit(solution)/shard_map/dot_general | solution.py:23
  153.5 1.9 collective-permute-start
  155.5 2.2 collective-permute-start.1
  157.7 4.7 convolution_bitcast_fusion.2
  162.4 4.7 negate_bitcast_fusion.2
  167.1 14.5 %convolution_bitcast_fusion.1 = f32[8,512,512]{2,1,0:T(8,128)} fusion(f32[8,256,512]{2,1,0:T(8,128)} %bitcast.80), kind=kOutput, calls=%fused_computation.21 | convolution fusion | flops 6444285952 | bytes 12582912 | tf_op jit(solution)/shard_map/fb,nbc->nfc/dot_general | solution.py:45
  181.6 11.1 %collective-permute-done.1 = bf16[1024,512]{1,0:T(8,128)(2,1)} collective-permute-done((bf16[1024,512]{1,0:T(8,128)(2,1)S(1)}, bf16[1024,512]{1,0:T(8,128)(2,1)}, u32[]{:S(2)}, u32[]{:S(2)}) %collective-permute-start.1) | collective-permute-done | bytes 1048608 | tf_op jit(solution)/shard_map/ppermute | solution.py:16
  194.3 5.7 %convolution_bitcast_fusion = f32[12,512,512]{1,2,0:T(8,128)S(1)} fusion(bf16[12,256,512]{2,1,0:T(8,128)(2,1)S(1)} %bitcast.78), kind=kOutput, calls=%fused_computation.18 | convolution fusion | flops 4833673216 | bytes 15728640 | tf_op jit(solution)/shard_map/fb,nbc->nfc/dot_general | solution.py:45
  200.0 9.9 %negate_bitcast_fusion = f32[12,512,512]{1,2,0:T(8,128)} fusion(bf16[12,256,512]{2,1,0:T(8,128)(2,1)S(1)} %bitcast.79), kind=kOutput, calls=%fused_computation.12 | convolution fusion | flops 4836818944 | bytes 15728640 | tf_op jit(solution)/shard_map/fb,nbc->nfc/dot_general | solution.py:46
  210.0 16.4 %fusion.4 = (f32[11,512,512]{1,2,0:T(8,128)}, f32[11,512,512]{1,2,0:T(8,128)}) fusion(f32[12,512,512]{1,2,0:T(8,128)} %negate_bitcast_fusion, f32[512]{0:T(512)S(1)} %fusion.39, f32[12,512,512]{1,2,0:T(8,128)S(1)} %convolution_bitcast_fusion), kind=kLoop, calls=%fused_computation.14 | loop fusion | flops 11534336 | bytes 69208064 | tf_op jit(solution)/shard_map/add | solution.py:58
  226.3 12.1 %copy.25 = f32[11,512,512]{2,1,0:T(8,128)} copy(f32[11,512,512]{1,2,0:T(8,128)} %get-tuple-element.369) | data formatting | bytes 23068672
  238.5 12.2 %copy.26 = f32[11,512,512]{2,1,0:T(8,128)} copy(f32[11,512,512]{1,2,0:T(8,128)} %get-tuple-element.368) | data formatting | bytes 23068672
  250.6 77.0 %while.33 = (s32[]{:T(128)}, f32[8,512,512]{2,1,0:T(8,128)}, f32[8,512,512]{2,1,0:T(8,128)}, f32[4,512,512]{2,1,0:T(8,128)}, f32[11,512,512]{2,1,0:T(8,128)}, /*...) while((s32[]{:T(128)}, f32[8,512,512]{2,1,0:T(8,128)}, ...), condition=%wide.region_3.4_spmd.clone, body=%wide.region_2.3_spmd.clone.sunk | while | flops 20971524 | bytes 56623212 | solution.py:90
  251.0 1.7 dynamic-slice_bitcast_fusion.7
  252.7 11.9 %fusion.96 = (f32[8,512,512]{2,1,0:T(8,128)}, f32[8,512,512]{2,1,0:T(8,128)}) fusion(f32[8,512,512]{2,1,0:T(8,128)} %get-tuple-element.510, f32[11,512,512]{2,1,0:T(8,128)} %get-tuple-element.523, s32[]{:T(128)} %get-tuple-element.508, f32[11,512,512]{2,1,0:T(8,128)} %get-tuple-element.521, f32[512,512]{1,0:T(8,128)S(1)} %get-tuple-element.468, ...), kind=kLoop, calls=%fused_computation.7.clone.1 | loop fusion | flops 20971520 | bytes 52428804 | tf_op jit(solution)/shard_map/while/body/eval_jaxpr/sub | solution.py:86
  264.6 1.7 dynamic-slice_bitcast_fusion.7
  266.4 19.3 %fusion.96 = (f32[8,512,512]{2,1,0:T(8,128)}, f32[8,512,512]{2,1,0:T(8,128)}) fusion(f32[8,512,512]{2,1,0:T(8,128)} %get-tuple-element.510, f32[11,512,512]{2,1,0:T(8,128)} %get-tuple-element.523, s32[]{:T(128)} %get-tuple-element.508, f32[11,512,512]{2,1,0:T(8,128)} %get-tuple-element.521, f32[512,512]{1,0:T(8,128)S(1)} %get-tuple-element.468, ...), kind=kLoop, calls=%fused_computation.7.clone.1 | loop fusion | flops 20971520 | bytes 52428804 | tf_op jit(solution)/shard_map/while/body/eval_jaxpr/sub | solution.py:86
  285.6 1.7 dynamic-slice_bitcast_fusion.7
  287.4 19.3 %fusion.96 = (f32[8,512,512]{2,1,0:T(8,128)}, f32[8,512,512]{2,1,0:T(8,128)}) fusion(f32[8,512,512]{2,1,0:T(8,128)} %get-tuple-element.510, f32[11,512,512]{2,1,0:T(8,128)} %get-tuple-element.523, s32[]{:T(128)} %get-tuple-element.508, f32[11,512,512]{2,1,0:T(8,128)} %get-tuple-element.521, f32[512,512]{1,0:T(8,128)S(1)} %get-tuple-element.468, ...), kind=kLoop, calls=%fused_computation.7.clone.1 | loop fusion | flops 20971520 | bytes 52428804 | tf_op jit(solution)/shard_map/while/body/eval_jaxpr/sub | solution.py:86
  306.7 1.7 dynamic-slice_bitcast_fusion.7
  308.4 19.3 %fusion.96 = (f32[8,512,512]{2,1,0:T(8,128)}, f32[8,512,512]{2,1,0:T(8,128)}) fusion(f32[8,512,512]{2,1,0:T(8,128)} %get-tuple-element.510, f32[11,512,512]{2,1,0:T(8,128)} %get-tuple-element.523, s32[]{:T(128)} %get-tuple-element.508, f32[11,512,512]{2,1,0:T(8,128)} %get-tuple-element.521, f32[512,512]{1,0:T(8,128)S(1)} %get-tuple-element.468, ...), kind=kLoop, calls=%fused_computation.7.clone.1 | loop fusion | flops 20971520 | bytes 52428804 | tf_op jit(solution)/shard_map/while/body/eval_jaxpr/sub | solution.py:86
  327.7 14.5 %fusion.15 = f32[8,512,256]{1,2,0:T(8,128)S(1)} fusion(f32[8,512,512]{2,1,0:T(8,128)} %get-tuple-element.254), kind=kOutput, calls=%fused_computation.38 | convolution fusion | flops 6444285952 | bytes 12582912 | tf_op jit(solution)/shard_map/fa,nfc->nac/dot_general | solution.py:50
  342.2 13.8 %subtract_multiply_fusion = f32[8,512,256]{1,2,0:T(8,128)} fusion(f32[8,512,256]{1,2,0:T(8,128)S(1)} %fusion.15, f32[8,512,512]{2,1,0:T(8,128)S(1)} %copy-done.2), kind=kOutput, calls=%fused_computation.19 | convolution fusion | flops 6446383104 | bytes 16777216 | tf_op jit(solution)/shard_map/fa,nfc->nac/dot_general | solution.py:51
  356.0 14.6 %negate_bitcast_fusion.1 = f32[8,512,512]{2,1,0:T(8,128)} fusion(f32[8,256,512]{2,1,0:T(8,128)} %bitcast.81), kind=kOutput, calls=%fused_computation.17 | convolution fusion | flops 6446383104 | bytes 12582912 | tf_op jit(solution)/shard_map/fb,nbc->nfc/dot_general | solution.py:46
  370.6 88.1 %while.32 = (s32[]{:T(128)}, f32[4,512,512]{2,1,0:T(8,128)}, f32[4,512,512]{2,1,0:T(8,128)}, f32[8,512,512]{2,1,0:T(8,128)}, f32[11,512,512]{2,1,0:T(8,128)}, /*...) while((s32[]{:T(128)}, f32[4,512,512]{2,1,0:T(8,128)}, ...), condition=%wide.region_1.2_spmd.clone, body=%wide.region_0.1_spmd.clone.sunk | while | flops 10485763 | bytes 31457388 | solution.py:77
  370.6 1.7 dynamic-slice_bitcast_fusion.6
  372.4 6.9 %fusion.95 = (f32[4,512,512]{2,1,0:T(8,128)}, f32[4,512,512]{2,1,0:T(8,128)}) fusion(f32[4,512,512]{2,1,0:T(8,128)} %get-tuple-element.483, f32[11,512,512]{2,1,0:T(8,128)} %get-tuple-element.496, s32[]{:T(128)} %get-tuple-element.481, f32[11,512,512]{2,1,0:T(8,128)} %get-tuple-element.494, f32[512,512]{1,0:T(8,128)S(1)} %get-tuple-element.457, ...), kind=kLoop, calls=%fused_computation.1.clone.1 | loop fusion | flops 10485760 | bytes 27262980 | tf_op jit(solution)/shard_map/while/body/eval_jaxpr/sub | solution.py:73
  379.3 1.7 dynamic-slice_bitcast_fusion.6
  381.0 9.8 %fusion.95 = (f32[4,512,512]{2,1,0:T(8,128)}, f32[4,512,512]{2,1,0:T(8,128)}) fusion(f32[4,512,512]{2,1,0:T(8,128)} %get-tuple-element.483, f32[11,512,512]{2,1,0:T(8,128)} %get-tuple-element.496, s32[]{:T(128)} %get-tuple-element.481, f32[11,512,512]{2,1,0:T(8,128)} %get-tuple-element.494, f32[512,512]{1,0:T(8,128)S(1)} %get-tuple-element.457, ...), kind=kLoop, calls=%fused_computation.1.clone.1 | loop fusion | flops 10485760 | bytes 27262980 | tf_op jit(solution)/shard_map/while/body/eval_jaxpr/sub | solution.py:73
  390.8 1.7 dynamic-slice_bitcast_fusion.6
  392.6 9.8 %fusion.95 = (f32[4,512,512]{2,1,0:T(8,128)}, f32[4,512,512]{2,1,0:T(8,128)}) fusion(f32[4,512,512]{2,1,0:T(8,128)} %get-tuple-element.483, f32[11,512,512]{2,1,0:T(8,128)} %get-tuple-element.496, s32[]{:T(128)} %get-tuple-element.481, f32[11,512,512]{2,1,0:T(8,128)} %get-tuple-element.494, f32[512,512]{1,0:T(8,128)S(1)} %get-tuple-element.457, ...), kind=kLoop, calls=%fused_computation.1.clone.1 | loop fusion | flops 10485760 | bytes 27262980 | tf_op jit(solution)/shard_map/while/body/eval_jaxpr/sub | solution.py:73
  402.3 1.7 dynamic-slice_bitcast_fusion.6
  404.1 9.7 %fusion.95 = (f32[4,512,512]{2,1,0:T(8,128)}, f32[4,512,512]{2,1,0:T(8,128)}) fusion(f32[4,512,512]{2,1,0:T(8,128)} %get-tuple-element.483, f32[11,512,512]{2,1,0:T(8,128)} %get-tuple-element.496, s32[]{:T(128)} %get-tuple-element.481, f32[11,512,512]{2,1,0:T(8,128)} %get-tuple-element.494, f32[512,512]{1,0:T(8,128)S(1)} %get-tuple-element.457, ...), kind=kLoop, calls=%fused_computation.1.clone.1 | loop fusion | flops 10485760 | bytes 27262980 | tf_op jit(solution)/shard_map/while/body/eval_jaxpr/sub | solution.py:73
  413.8 1.7 dynamic-slice_bitcast_fusion.6
  415.5 9.6 %fusion.95 = (f32[4,512,512]{2,1,0:T(8,128)}, f32[4,512,512]{2,1,0:T(8,128)}) fusion(f32[4,512,512]{2,1,0:T(8,128)} %get-tuple-element.483, f32[11,512,512]{2,1,0:T(8,128)} %get-tuple-element.496, s32[]{:T(128)} %get-tuple-element.481, f32[11,512,512]{2,1,0:T(8,128)} %get-tuple-element.494, f32[512,512]{1,0:T(8,128)S(1)} %get-tuple-element.457, ...), kind=kLoop, calls=%fused_computation.1.clone.1 | loop fusion | flops 10485760 | bytes 27262980 | tf_op jit(solution)/shard_map/while/body/eval_jaxpr/sub | solution.py:73
  425.1 1.7 dynamic-slice_bitcast_fusion.6
  426.8 9.4 %fusion.95 = (f32[4,512,512]{2,1,0:T(8,128)}, f32[4,512,512]{2,1,0:T(8,128)}) fusion(f32[4,512,512]{2,1,0:T(8,128)} %get-tuple-element.483, f32[11,512,512]{2,1,0:T(8,128)} %get-tuple-element.496, s32[]{:T(128)} %get-tuple-element.481, f32[11,512,512]{2,1,0:T(8,128)} %get-tuple-element.494, f32[512,512]{1,0:T(8,128)S(1)} %get-tuple-element.457, ...), kind=kLoop, calls=%fused_computation.1.clone.1 | loop fusion | flops 10485760 | bytes 27262980 | tf_op jit(solution)/shard_map/while/body/eval_jaxpr/sub | solution.py:73
  436.2 1.7 dynamic-slice_bitcast_fusion.6
  438.0 9.4 %fusion.95 = (f32[4,512,512]{2,1,0:T(8,128)}, f32[4,512,512]{2,1,0:T(8,128)}) fusion(f32[4,512,512]{2,1,0:T(8,128)} %get-tuple-element.483, f32[11,512,512]{2,1,0:T(8,128)} %get-tuple-element.496, s32[]{:T(128)} %get-tuple-element.481, f32[11,512,512]{2,1,0:T(8,128)} %get-tuple-element.494, f32[512,512]{1,0:T(8,128)S(1)} %get-tuple-element.457, ...), kind=kLoop, calls=%fused_computation.1.clone.1 | loop fusion | flops 10485760 | bytes 27262980 | tf_op jit(solution)/shard_map/while/body/eval_jaxpr/sub | solution.py:73
  447.4 1.7 dynamic-slice_bitcast_fusion.6
  449.1 9.4 %fusion.95 = (f32[4,512,512]{2,1,0:T(8,128)}, f32[4,512,512]{2,1,0:T(8,128)}) fusion(f32[4,512,512]{2,1,0:T(8,128)} %get-tuple-element.483, f32[11,512,512]{2,1,0:T(8,128)} %get-tuple-element.496, s32[]{:T(128)} %get-tuple-element.481, f32[11,512,512]{2,1,0:T(8,128)} %get-tuple-element.494, f32[512,512]{1,0:T(8,128)S(1)} %get-tuple-element.457, ...), kind=kLoop, calls=%fused_computation.1.clone.1 | loop fusion | flops 10485760 | bytes 27262980 | tf_op jit(solution)/shard_map/while/body/eval_jaxpr/sub | solution.py:73
  458.7 8.2 %fusion.17 = f32[4,512,256]{1,2,0:T(8,128)S(1)} fusion(f32[4,512,512]{2,1,0:T(8,128)} %get-tuple-element.252), kind=kOutput, calls=%fused_computation.40 | convolution fusion | flops 3223060480 | bytes 6291456 | tf_op jit(solution)/shard_map/fa,nfc->nac/dot_general | solution.py:50
  466.9 7.0 %multiply_convert_fusion = bf16[4,512,256]{1,2,0:T(8,128)(2,1)} fusion(f32[4,512,256]{1,2,0:T(8,128)S(1)} %fusion.17, f32[4,512,512]{2,1,0:T(8,128)S(1)} %copy-done.3), kind=kOutput, calls=%fused_computation.24 | convolution fusion | flops 3224633344 | bytes 7340032 | tf_op jit(solution)/shard_map/fa,nfc->nac/dot_general | solution.py:51
  473.9 1.7 broadcast_multiply_fusion
  (21 shorter events, 2.3 us)
Async XLA Ops:
  7.2 150.5 %copy-start = (bf16[1024,512]{1,0:T(8,128)(2,1)S(1)}, bf16[1024,512]{1,0:T(8,128)(2,1)}, u32[]{:S(2)}) copy-start(bf16[1024,512]{1,0:T(8,128)(2,1)} %param.8) | copy-start | bytes 3145732
  13.1 131.3 %all-to-all-start = ((bf16[8,1024,512]{1,2,0:T(8,128)(2,1)}), bf16[8,1024,512]{1,2,0:T(8,128)(2,1)}, u32[]{:S(2)}, u32[]{:S(2)}) async-start(bf16[8,1024,512]{1,2,0:T(8,128)(2,1)} %stack.2), calls=%async_computation | async-start | bytes 16777216 | tf_op jit(solution)/shard_map/all_to_all | solution.py:25
  20.3 146.9 %all-gather.2.cloned.1.call-start = ((), (), s32[]{:S(2)}) async-start(), calls=%async_computation.2 | async-start | bytes 4456448 | tf_op jit(solution)/shard_map/all_gather | solution.py:32
  21.0 453.0 %reduce-scatter.2.cloned.1.call-start = ((), (), s32[]{:S(2)}) async-start(), calls=%async_computation.3 | async-start | bytes 4456448 | tf_op jit(solution)/shard_map/reduce_scatter | solution.py:95
  153.5 28.1 %collective-permute-start = (bf16[1024,512]{1,0:T(8,128)(2,1)S(1)}, bf16[1024,512]{1,0:T(8,128)(2,1)S(1)}, u32[]{:S(2)}, u32[]{:S(2)}) collective-permute-start(bf16[1024,512]{1,0:T(8,128)(2,1)S(1)} %convolution_convert_fusion), channel_id=1, source_target_pairs={{8,0},{16,8},{24,16},{32,24},{40,32},{48,40},{56,48},{64,56},{72,6... | collective-permute-start | bytes 3145736 | tf_op jit(solution)/shard_map/ppermute | solution.py:16
  155.5 37.3 %collective-permute-start.1 = (bf16[1024,512]{1,0:T(8,128)(2,1)S(1)}, bf16[1024,512]{1,0:T(8,128)(2,1)}, u32[]{:S(2)}, u32[]{:S(2)}) collective-permute-start(bf16[1024,512]{1,0:T(8,128)(2,1)S(1)} %convolution_convert_fusion), channel_id=1, source_target_pairs={{16,0},{24,8},{32,16},{40,24},{48,32},{56,40},{64,48},{72,56},{80,... | collective-permute-start | bytes 3145736 | tf_op jit(solution)/shard_map/ppermute | solution.py:16
  327.7 14.6 %copy-start.2 = (f32[8,512,512]{2,1,0:T(8,128)S(1)}, f32[8,512,512]{2,1,0:T(8,128)}, u32[]{:S(2)}) copy-start(f32[8,512,512]{2,1,0:T(8,128)} %get-tuple-element.255) | copy-start | bytes 25165828
  458.7 8.2 %copy-start.3 = (f32[4,512,512]{2,1,0:T(8,128)S(1)}, f32[4,512,512]{2,1,0:T(8,128)}, u32[]{:S(2)}) copy-start(f32[4,512,512]{2,1,0:T(8,128)} %get-tuple-element.253) | copy-start | bytes 12582916
  458.7 16.9 %copy-start.1 = (bf16[1024,512]{1,0:T(8,128)(2,1)S(1)}, bf16[1024,512]{1,0:T(8,128)(2,1)}, u32[]{:S(2)}) copy-start(bf16[1024,512]{1,0:T(8,128)(2,1)} %param.8) | copy-start | bytes 3145732
Sparse Core Ops, SparseCore 0:
  22.8 106.9 all-gather.1
  356.1 66.6 reduce-scatter.1
